TPU v7x, 32 devices: a whole 2x2x4 slice. The times are simulated.
32 devices in a mesh: tm: 2 (over y), gy: 4 (over z), gz: 4 (over x, core).
Axes of the slice: x: 2, y: 2, z: 4, core: 2. Of those that a mesh axis runs over, the one named last changes fastest.
Arguments:
- inverse_mass: float32 [32, 64, 128], P('gy', 'gz'), may hold values from 0.5 to 2
- actuator_of_cell: int32 [32, 64, 128], P('gy', 'gz'), may hold values from 0 to 31
- plan_ids: int32 [2, 32], P('tm'), may hold values from 0 to 15
- profiles: float32 [16, 9], replicated, may hold values from -4 to 4
- directions: float32 [3, 32], replicated, may hold values from -4 to 4
Outputs:
- predicted_state: float32 [2, 6, 32, 64, 128], P('tm', None, 'gy', 'gz')
All inputs are finite; a program needn't handle non-finite values.
Results may differ from a plain program's by a relative error of at most 0.00021.
Values sent between devices are 32-bit elements; how exact they have to be, the bound alone decides.
A program may use at most 64 MiB of HBM per device.

v0:
```python
import functools
import math

import jax
import jax.numpy as jnp
import numpy as np
from jax import lax
from jax.experimental import pallas as pl
from jax.experimental.pallas import tpu as pltpu
from jax.sharding import PartitionSpec as P

STEPS = 8
TERMS = 8
LANES = 128
MESH = pl.DeviceIdType.MESH

lame_ratio = 2.5
mass_top = 2.0
step_squared = 1.0


def cheb_tables():
    spectrum_top = mass_top * 12.0 * (1.0 + lame_ratio)
    time_step = math.sqrt(step_squared / spectrum_top)
    horizon = STEPS * time_step
    angles = np.pi * (np.arange(TERMS) + 0.5) / TERMS
    node_x = 0.5 * spectrum_top * (1.0 + np.cos(angles))
    node_root = np.sqrt(node_x)
    values_c = np.cos(horizon * node_root)
    values_s = np.sin(horizon * node_root) / node_root
    values_g = node_root * np.sin(horizon * node_root)

    def project_values(values):
        result = np.array([2.0 / TERMS * np.sum(values * np.cos(k * angles)) for k in range(TERMS)])
        result[0] = 0.5 * result[0]
        return [float(entry) for entry in result]

    return (
        spectrum_top,
        time_step,
        project_values(values_c),
        project_values(values_s),
        project_values(values_g),
    )


def down(field, first):
    rows = lax.broadcasted_iota(jnp.int32, field.shape, 0)
    return jnp.where(rows == 0, first, pltpu.roll(field, 1, 0))


def up(field, last):
    size = field.shape[0]
    rows = lax.broadcasted_iota(jnp.int32, field.shape, 0)
    return jnp.where(rows == size - 1, last, pltpu.roll(field, size - 1, 0))


def x_down(field, first):
    lanes = lax.broadcasted_iota(jnp.int32, field.shape, 1)
    return jnp.where(lanes == 0, first, pltpu.roll(field, 1, 1))


def x_up(field):
    size = field.shape[1]
    lanes = lax.broadcasted_iota(jnp.int32, field.shape, 1)
    return jnp.where(lanes == size - 1, 0.0, pltpu.roll(field, size - 1, 1))


def kernel(
    sizes,
    mass_ref,
    act_ref,
    table_ref,
    coef_ref,
    out_ref,
    tabs,
    tab_rows,
    amp,
    force,
    disp,
    vel,
    cheb,
    y_in,
    z_in,
    d_in,
    send_sem,
    recv_sem,
    tab_send,
    tab_recv,
):
    count_t, count_y, count_z, windows, count_act = sizes
    size_y, size_z, size_x = mass_ref.shape
    spectrum_top, time_step, _, _, _ = cheb_tables()
    scale = 2.0 / spectrum_top
    at_t, at_y, at_z = (lax.axis_index(name) for name in ("tm", "gy", "gz"))
    has_low_y, has_high_y = at_y > 0, at_y < count_y - 1
    has_low_z, has_high_z = at_z > 0, at_z < count_z - 1
    beside = [
        (has_low_y, {"gy": at_y - 1}),
        (has_high_y, {"gy": at_y + 1}),
        (has_low_z, {"gz": at_z - 1}),
        (has_high_z, {"gz": at_z + 1}),
        (jnp.logical_and(has_low_y, has_high_z), {"gy": at_y - 1, "gz": at_z + 1}),
        (jnp.logical_and(has_high_y, has_low_z), {"gy": at_y + 1, "gz": at_z - 1}),
    ]
    later = [(at_t + s < count_t, {"tm": at_t + s}) for s in range(1, windows)]
    earlier = [(at_t - s >= 0, {"tm": at_t - s}) for s in range(1, windows)]

    y_in[...] = jnp.zeros_like(y_in)
    z_in[...] = jnp.zeros_like(z_in)
    d_in[...] = jnp.zeros_like(d_in)
    tabs[...] = jnp.zeros_like(tabs)

    barrier = pltpu.get_barrier_semaphore()
    everyone = beside + later + earlier
    for exists, device in everyone:

        @pl.when(exists)
        def _(device=device):
            pl.semaphore_signal(barrier, inc=1, device_id=device, device_id_type=MESH)

    peers = 0
    for exists, _ in everyone:
        peers = peers + jnp.where(exists, 1, 0)
    pl.semaphore_wait(barrier, peers)

    def table_copy(s, device):
        return pltpu.make_async_remote_copy(
            src_ref=table_ref,
            dst_ref=tabs.at[s - 1],
            send_sem=tab_send.at[s - 1],
            recv_sem=tab_recv.at[s - 1],
            device_id=device,
            device_id_type=MESH,
        )

    for s in range(1, windows):
        exists, device = later[s - 1]

        @pl.when(exists)
        def _(s=s, device=device):
            table_copy(s, device).start()

    def spread(s, table):
        for a in range(count_act):
            tab_rows[s, a] = jnp.broadcast_to(table[:, a : a + 1], table.shape)

    spread(0, table_ref[...])
    for s in range(1, windows):
        exists, device = later[s - 1]
        here, source = earlier[s - 1]

        @pl.when(here)
        def _(s=s, source=source):
            table_copy(s, source).wait_recv()

        spread(s, tabs[s - 1])

        @pl.when(exists)
        def _(s=s, device=device):
            table_copy(s, device).wait_send()

    times = STEPS + 1
    entries = [(s, n) for s in range(windows) for n in range(times)]
    entries += [(0, times + c) for c in range(3)]

    def look_up(y, carry):
        act = act_ref[y]
        mass = mass_ref[y]

        def one(a, values):
            hit = act == a
            return tuple(
                jnp.where(hit, tab_rows[s, a, r : r + 1, :], value)
                for (s, r), value in zip(entries, values)
            )

        zero = jnp.zeros((size_z, size_x), jnp.float32)
        values = lax.fori_loop(0, count_act, one, tuple(zero for _ in entries))
        for (s, r), value in zip(entries, values):
            if r < times:
                amp[s, r, y] = value
        for c in range(3):
            force[c, y] = mass * values[windows * times + c]
        for s in range(windows):
            for c in range(3):
                half = (0.5 * time_step) * (force[c, y] * values[s * times])
                vel[s, c, y] = half
                disp[0, s, c, y] = time_step * half
        return carry

    lax.fori_loop(0, size_y, look_up, 0)

    def copies(field, states, slot):
        top, end = size_y - 1, size_z - 1
        pairs = [
            (field.at[:, :, 0:1], y_in.at[slot, 1, 0:states]),
            (field.at[:, :, top : top + 1], y_in.at[slot, 0, 0:states]),
            (field.at[:, :, :, 0:1], z_in.at[slot, 1, 0:states]),
            (field.at[:, :, :, end : end + 1], z_in.at[slot, 0, 0:states]),
            (field.at[:, 0:1, 0:1, end : end + 1], d_in.at[slot, 1, 0:states]),
            (field.at[:, 1:2, top : top + 1, 0:1], d_in.at[slot, 0, 0:states]),
        ]
        opposite = (1, 0, 3, 2, 5, 4)
        made = []
        for i, ((source, target), (exists, device)) in enumerate(zip(pairs, beside)):
            made.append(
                (
                    exists,
                    pltpu.make_async_remote_copy(
                        src_ref=source,
                        dst_ref=target,
                        send_sem=send_sem.at[slot, i],
                        recv_sem=recv_sem.at[slot, opposite[i]],
                        device_id=device,
                        device_id_type=MESH,
                    ),
                )
            )
        return made

    def start(field, states, slot):
        for exists, copy in copies(field, states, slot):

            @pl.when(exists)
            def _(copy=copy):
                copy.start()

    def finish(field, states, slot):
        made = copies(field, states, slot)
        for i in range(6):
            exists = beside[i][0]

            @pl.when(exists)
            def _(i=i):
                made[(1, 0, 3, 2, 5, 4)[i]][1].wait_recv()

        for exists, copy in made:

            @pl.when(exists)
            def _(copy=copy):
                copy.wait_send()

    def stiffness(field, s, slot, use):
        def get(c, y):
            if y < 0:
                return y_in[slot, 0, s, c, 0]
            if y == size_y:
                return y_in[slot, 1, s, c, 0]
            return field[s, c, y]

        def divergence(y, u_y, u_z, u_x, above_y, last_z):
            value = (above_y - u_y) + (up(u_z, last_z) - u_z)
            return value + (x_up(u_x) - u_x)

        u_low = [get(c, -1) for c in range(3)]
        u = [get(c, 0) for c in range(3)]
        corner = d_in[slot, 0, s, 0, 0]
        p_low = divergence(-1, u_low[0], u_low[1], u_low[2], u[0], corner)
        for y in range(size_y):
            u_high = [get(c, y + 1) for c in range(3)]
            z_low = [z_in[slot, 0, s, c, y] for c in range(3)]
            z_high = [z_in[slot, 1, s, c, y] for c in range(3)]
            if y < size_y - 1:
                z_low_above = z_in[slot, 0, s, 0, y + 1]
            else:
                z_low_above = d_in[slot, 1, s, 0, 0]
            u_ups = up(u[1], z_high[1])
            x_ups = x_up(u[2])
            p = ((u_high[0] - u[0]) + (u_ups - u[1])) + (x_ups - u[2])
            p_edge = (z_low_above - z_low[0]) + (u[1][0:1] - z_low[1])
            p_edge = p_edge + (x_up(z_low[2]) - z_low[2])
            inner = [p_low - p, down(p, p_edge) - p, x_down(p, u[2]) - p]
            mass = mass_ref[y]
            for c in range(3):
                total = u_high[c] + u_low[c]
                z_up = u_ups if c == 1 else up(u[c], z_high[c])
                total = total + (z_up + down(u[c], z_low[c]))
                xs = x_ups if c == 2 else x_up(u[c])
                total = total + (xs + x_down(u[c], 0.0))
                use(c, y, u[c], mass * ((6.0 * u[c] - total) + lame_ratio * inner[c]))
            u_low, u, p_low = u, u_high, p

    def forced(n, carry):
        slot = lax.rem(n, 2)
        other = 1 - slot
        field = disp.at[slot]
        start(field, windows, slot)
        is_last = n == STEPS - 1
        kick = jnp.where(is_last, 0.5 * time_step, time_step).astype(jnp.float32)
        drift = jnp.where(is_last, 0.0, time_step).astype(jnp.float32)
        finish(field, windows, slot)
        for s in range(windows):

            def use(c, y, u, stiff, s=s):
                half = vel[s, c, y] + kick * (force[c, y] * amp[s, n + 1, y] - stiff)
                vel[s, c, y] = half
                disp[other, s, c, y] = u + drift * half

            stiffness(field, s, slot, use)
        return carry

    lax.fori_loop(0, STEPS, forced, 0)
    final = STEPS % 2

    out_ref[0, 0:3] = disp[final, 0]
    out_ref[0, 3:6] = vel[0]
    if windows > 1:
        cheb[0, 0] = disp[final, windows - 1]
        cheb[0, 1] = vel[windows - 1]

    def add_term(k, slot, goal_u, goal_v):
        cc, cs, cg = coef_ref[0, k], coef_ref[1, k], coef_ref[2, k]
        for c in range(3):
            for y in range(size_y):
                t_u, t_v = cheb[slot, 0, c, y], cheb[slot, 1, c, y]
                goal_u[c, y] = goal_u[c, y] + (cc * t_u + cs * t_v)
                goal_v[c, y] = goal_v[c, y] + (cc * t_v - cg * t_u)

    base = STEPS
    for w in range(windows - 1, 0, -1):
        if w == 1:
            goal_u, goal_v = out_ref.at[0, 0:3], out_ref.at[0, 3:6]
        else:
            goal_u, goal_v = disp.at[final, w - 1], vel.at[w - 1]
        cheb[1] = jnp.zeros(cheb.shape[1:], jnp.float32)

        def term(k, carry, base=base, goal_u=goal_u, goal_v=goal_v):
            slot = lax.rem(k, 2)
            other = 1 - slot
            wire = lax.rem(k + base, 2)
            field = cheb.at[slot]
            start(field, 2, wire)
            add_term(k, slot, goal_u, goal_v)
            lead = jnp.where(k == 0, 1.0, 2.0).astype(jnp.float32)
            finish(field, 2, wire)
            for s in range(2):

                def use(c, y, u, stiff, s=s):
                    cheb[other, s, c, y] = lead * (scale * stiff - u) - cheb[other, s, c, y]

                stiffness(field, s, wire, use)
            return carry

        lax.fori_loop(0, TERMS - 1, term, 0)
        add_term(TERMS - 1, (TERMS - 1) % 2, goal_u, goal_v)
        base += TERMS - 1
        if w > 1:
            cheb[0, 0] = disp[final, w - 1]
            cheb[0, 1] = vel[w - 1]


def body(counts, inverse_mass, actuator_of_cell, plan_ids, profiles, directions):
    size_y, size_z, size_x = inverse_mass.shape
    count_act = directions.shape[1]
    count_prof, times = profiles.shape
    windows = min(counts[0], 3)
    wide = -(-count_act // LANES) * LANES
    rows = -(-(times + 3) // 8) * 8
    picked = plan_ids[0][None, None, :] == jnp.arange(count_prof, dtype=jnp.int32)[None, :, None]
    chosen = jnp.sum(jnp.where(picked, profiles.T[:, :, None], 0.0), axis=1)
    table = jnp.concatenate([chosen, directions], axis=0)
    table = jnp.pad(table, ((0, rows - times - 3), (0, wide - count_act)))
    _, _, coef_c, coef_s, coef_g = cheb_tables()
    coefs = jnp.asarray(np.array([coef_c, coef_s, coef_g], np.float32))
    block = (size_y, size_z, size_x)
    most = max(windows, 2)
    f32 = jnp.float32
    vmem = pl.BlockSpec(memory_space=pltpu.VMEM)
    return pl.pallas_call(
        functools.partial(kernel, counts + (windows, count_act)),
        out_shape=jax.ShapeDtypeStruct((1, 6) + block, f32),
        in_specs=[vmem, vmem, vmem, pl.BlockSpec(memory_space=pltpu.SMEM)],
        out_specs=vmem,
        scratch_shapes=[
            pltpu.VMEM((most - 1, rows, wide), f32),
            pltpu.VMEM((windows, count_act, rows, size_x), f32),
            pltpu.VMEM((windows, times) + block, f32),
            pltpu.VMEM((3,) + block, f32),
            pltpu.VMEM((2, windows, 3) + block, f32),
            pltpu.VMEM((windows, 3) + block, f32),
            pltpu.VMEM((2, 2, 3) + block, f32),
            pltpu.VMEM((2, 2, most, 3, 1, size_z, size_x), f32),
            pltpu.VMEM((2, 2, most, 3, size_y, 1, size_x), f32),
            pltpu.VMEM((2, 2, most, 1, 1, 1, size_x), f32),
            pltpu.SemaphoreType.DMA((2, 6)),
            pltpu.SemaphoreType.DMA((2, 6)),
            pltpu.SemaphoreType.DMA((most - 1,)),
            pltpu.SemaphoreType.DMA((most - 1,)),
        ],
        compiler_params=pltpu.CompilerParams(
            collective_id=0, has_side_effects=True, vmem_limit_bytes=32 * 1024 * 1024
        ),
    )(inverse_mass, actuator_of_cell, table, coefs)


def solution(mesh):
    counts = (mesh.shape["tm"], mesh.shape["gy"], mesh.shape["gz"])
    in_specs = (P("gy", "gz", None), P("gy", "gz", None), P("tm", None), P(), P())
    out_specs = P("tm", None, "gy", "gz", None)
    return jax.shard_map(
        functools.partial(body, counts),
        mesh=mesh,
        in_specs=in_specs,
        out_specs=out_specs,
        check_vma=False,
    )
```

profile of v0, /device:TPU:0, one launch (start us, length us, event | category | flops | bytes accessed | tf_op | source)
XLA Modules:
  0.0 79.6 jit_solution(8253006058886208425)
XLA Ops:
  0.0 0.0 copy-start.4
  0.0 0.7 copy-done.4
  0.7 0.8 copy.8
  1.4 0.0 copy-start.3
  1.4 0.1 select_reduce_fusion
  1.5 0.6 copy-done.3
  2.1 0.0 copy-start.2
  2.1 0.7 copy-done.2
  2.8 0.0 copy-start
  2.8 0.8 %copy-done = f32[8,16,128]{2,1,0:T(8,128)S(1)} copy-done((f32[8,16,128]{2,1,0:T(8,128)S(1)}, f32[8,16,128]{2,1,0:T(8,128)}, u32[]{:S(2)}) %copy-start) | copy-done | bytes 65560
  3.6 0.0 copy-start.1
  3.6 0.8 %copy-done.1 = s32[8,16,128]{2,1,0:T(8,128)S(1)} copy-done((s32[8,16,128]{2,1,0:T(8,128)S(1)}, s32[8,16,128]{2,1,0:T(8,128)}, u32[]{:S(2)}) %copy-start.1) | copy-done | bytes 65560
  4.5 74.4 %shard_map.67 = f32[1,6,8,16,128]{4,3,2,1,0:T(8,128)S(1)} custom-call(f32[8,16,128]{2,1,0:T(8,128)S(1)} %copy-done, s32[8,16,128]{2,1,0:T(8,128)S(1)} %copy-done.1, f32[16,128]{1,0:T(8,128)S(1)} %select_maximum_fusion.table_ref, f32[3,8]{1,0:T(4,128)S(1)} %copy-done.2), custom_call_target="tpu_custom_call" | custom-call | tf_op jit(solution)/shard_map/pallas_call | solution.py:370
  78.9 0.7 copy.10
  (2 shorter events, 0.0 us)
Async XLA Ops:
  0.0 0.7 copy-start.4
  1.4 0.7 copy-start.3
  2.1 0.7 copy-start.2
  2.8 0.8 %copy-start = (f32[8,16,128]{2,1,0:T(8,128)S(1)}, f32[8,16,128]{2,1,0:T(8,128)}, u32[]{:S(2)}) copy-start(f32[8,16,128]{2,1,0:T(8,128)} %mass_ref.1) | copy-start | bytes 196612
  3.6 0.8 %copy-start.1 = (s32[8,16,128]{2,1,0:T(8,128)S(1)}, s32[8,16,128]{2,1,0:T(8,128)}, u32[]{:S(2)}) copy-start(s32[8,16,128]{2,1,0:T(8,128)} %act_ref.1) | copy-start | bytes 196612
where the time goes:
time: 79.9 us; the launch traced here: 79.6 us
  Pallas kernels  74.4 us (93%)
  local copies, waits for them, and re-layouts  5.11 us (6%)
    pallas_call x1, Pallas kernels, body(): pl.pallas_call(functools.partial(kernel, counts + (windows, count_act)),...  74.4 us
    unnamed x11, local copies, waits for them, and re-layouts  4.33 us

commit v1 on v0

--- a/solution.py
+++ b/solution.py
@@ -191,15 +191,15 @@
 
     lax.fori_loop(0, size_y, look_up, 0)
 
-    def copies(field, states, slot):
+    def copies(field, s, slot):
         top, end = size_y - 1, size_z - 1
         pairs = [
-            (field.at[:, :, 0:1], y_in.at[slot, 1, 0:states]),
-            (field.at[:, :, top : top + 1], y_in.at[slot, 0, 0:states]),
-            (field.at[:, :, :, 0:1], z_in.at[slot, 1, 0:states]),
-            (field.at[:, :, :, end : end + 1], z_in.at[slot, 0, 0:states]),
-            (field.at[:, 0:1, 0:1, end : end + 1], d_in.at[slot, 1, 0:states]),
-            (field.at[:, 1:2, top : top + 1, 0:1], d_in.at[slot, 0, 0:states]),
+            (field.at[:, 0:1], y_in.at[slot, 1, s]),
+            (field.at[:, top : top + 1], y_in.at[slot, 0, s]),
+            (field.at[:, :,  0:1], z_in.at[slot, 1, s]),
+            (field.at[:, :,  end : end + 1], z_in.at[slot, 0, s]),
+            (field.at[0:1, 0:1, end : end + 1], d_in.at[slot, 1, s]),
+            (field.at[1:2, top : top + 1, 0:1], d_in.at[slot, 0, s]),
         ]
         opposite = (1, 0, 3, 2, 5, 4)
         made = []
@@ -210,8 +210,8 @@
                     pltpu.make_async_remote_copy(
                         src_ref=source,
                         dst_ref=target,
-                        send_sem=send_sem.at[slot, i],
-                        recv_sem=recv_sem.at[slot, opposite[i]],
+                        send_sem=send_sem.at[slot, s, i],
+                        recv_sem=recv_sem.at[slot, s, opposite[i]],
                         device_id=device,
                         device_id_type=MESH,
                     ),
@@ -219,15 +219,15 @@
             )
         return made
 
-    def start(field, states, slot):
-        for exists, copy in copies(field, states, slot):
+    def start(field, s, slot):
+        for exists, copy in copies(field, s, slot):
 
             @pl.when(exists)
             def _(copy=copy):
                 copy.start()
 
-    def finish(field, states, slot):
-        made = copies(field, states, slot)
+    def finish(field, s, slot):
+        made = copies(field, s, slot)
         for i in range(6):
             exists = beside[i][0]
 
@@ -285,11 +285,9 @@
         slot = lax.rem(n, 2)
         other = 1 - slot
         field = disp.at[slot]
-        start(field, windows, slot)
         is_last = n == STEPS - 1
         kick = jnp.where(is_last, 0.5 * time_step, time_step).astype(jnp.float32)
         drift = jnp.where(is_last, 0.0, time_step).astype(jnp.float32)
-        finish(field, windows, slot)
         for s in range(windows):
 
             def use(c, y, u, stiff, s=s):
@@ -297,9 +295,17 @@
                 vel[s, c, y] = half
                 disp[other, s, c, y] = u + drift * half
 
+            finish(disp.at[slot, s], s, slot)
             stiffness(field, s, slot, use)
+
+            @pl.when(n < STEPS - 1)
+            def _(s=s):
+                start(disp.at[other, s], s, other)
+
         return carry
 
+    for s in range(windows):
+        start(disp.at[0, s], s, 0)
     lax.fori_loop(0, STEPS, forced, 0)
     final = STEPS % 2
 
@@ -330,18 +336,24 @@
             other = 1 - slot
             wire = lax.rem(k + base, 2)
             field = cheb.at[slot]
-            start(field, 2, wire)
             add_term(k, slot, goal_u, goal_v)
             lead = jnp.where(k == 0, 1.0, 2.0).astype(jnp.float32)
-            finish(field, 2, wire)
             for s in range(2):
 
                 def use(c, y, u, stiff, s=s):
                     cheb[other, s, c, y] = lead * (scale * stiff - u) - cheb[other, s, c, y]
 
+                finish(cheb.at[slot, s], s, wire)
                 stiffness(field, s, wire, use)
+
+                @pl.when(k < TERMS - 2)
+                def _(s=s):
+                    start(cheb.at[other, s], s, 1 - wire)
+
             return carry
 
+        for s in range(2):
+            start(cheb.at[0, s], s, base % 2)
         lax.fori_loop(0, TERMS - 1, term, 0)
         add_term(TERMS - 1, (TERMS - 1) % 2, goal_u, goal_v)
         base += TERMS - 1
@@ -383,8 +395,8 @@
             pltpu.VMEM((2, 2, most, 3, 1, size_z, size_x), f32),
             pltpu.VMEM((2, 2, most, 3, size_y, 1, size_x), f32),
             pltpu.VMEM((2, 2, most, 1, 1, 1, size_x), f32),
-            pltpu.SemaphoreType.DMA((2, 6)),
-            pltpu.SemaphoreType.DMA((2, 6)),
+            pltpu.SemaphoreType.DMA((2, most, 6)),
+            pltpu.SemaphoreType.DMA((2, most, 6)),
             pltpu.SemaphoreType.DMA((most - 1,)),
             pltpu.SemaphoreType.DMA((most - 1,)),
         ],

time: 79.9 us -> 66 us (0.83)
  Pallas kernels: 74.4 us -> 60.5 us
    pallas_call x1, Pallas kernels: 74.4 us -> 60.5 us  [body(): pl.pallas_call(functools.partial(kernel, counts + (windows, count_act)),...]
where the time goes in v1:
time: 66 us; the launch traced here: 65.7 us
  Pallas kernels  60.5 us (92%)
  local copies, waits for them, and re-layouts  5.11 us (8%)
    pallas_call x1, Pallas kernels, body(): pl.pallas_call(functools.partial(kernel, counts + (windows, count_act)),...  60.5 us
    unnamed x11, local copies, waits for them, and re-layouts  4.33 us

profile of v1, /device:TPU:0, one launch (start us, length us, event | category | flops | bytes accessed | tf_op | source)
XLA Modules:
  0.0 65.7 jit_solution(13010358822088992644)
XLA Ops:
  0.0 0.0 copy-start.4
  0.0 0.7 copy-done.4
  0.7 0.8 %copy.8 = f32[9,16]{1,0:T(8,128)S(1)} copy(f32[9,16]{0,1:T(8,128)} %bitcast.2) | data formatting | bytes 1152 | tf_op jit(solution)/shard_map/transpose | solution.py:373
  1.4 0.0 copy-start.3
  1.4 0.1 select_reduce_fusion
  1.5 0.6 copy-done.3
  2.1 0.0 copy-start.2
  2.1 0.7 %copy-done.2 = f32[3,8]{1,0:T(4,128)S(1)} copy-done((f32[3,8]{1,0:T(4,128)S(1)}, f32[3,8]{1,0:T(4,128)}, u32[]{:S(2)}) %copy-start.2) | copy-done | bytes 120
  2.8 0.0 copy-start
  2.8 0.8 %copy-done = f32[8,16,128]{2,1,0:T(8,128)S(1)} copy-done((f32[8,16,128]{2,1,0:T(8,128)S(1)}, f32[8,16,128]{2,1,0:T(8,128)}, u32[]{:S(2)}) %copy-start) | copy-done | bytes 65560
  3.6 0.0 copy-start.1
  3.6 0.8 %copy-done.1 = s32[8,16,128]{2,1,0:T(8,128)S(1)} copy-done((s32[8,16,128]{2,1,0:T(8,128)S(1)}, s32[8,16,128]{2,1,0:T(8,128)}, u32[]{:S(2)}) %copy-start.1) | copy-done | bytes 65560
  4.5 60.5 %shard_map.67 = f32[1,6,8,16,128]{4,3,2,1,0:T(8,128)S(1)} custom-call(f32[8,16,128]{2,1,0:T(8,128)S(1)} %copy-done, s32[8,16,128]{2,1,0:T(8,128)S(1)} %copy-done.1, f32[16,128]{1,0:T(8,128)S(1)} %select_maximum_fusion.table_ref, f32[3,8]{1,0:T(4,128)S(1)} %copy-done.2), custom_call_target="tpu_custom_call" | custom-call | tf_op jit(solution)/shard_map/pallas_call | solution.py:382
  65.0 0.7 %copy.10 = f32[1,6,8,16,128]{4,3,2,1,0:T(8,128)} copy(f32[1,6,8,16,128]{4,3,2,1,0:T(8,128)S(1)} %shard_map.67) | data formatting | bytes 786432
  (2 shorter events, 0.0 us)
Async XLA Ops:
  0.0 0.7 copy-start.4
  1.4 0.7 %copy-start.3 = (f32[3,32]{1,0:T(4,128)S(1)}, f32[3,32]{1,0:T(4,128)}, u32[]{:S(2)}) copy-start(f32[3,32]{1,0:T(4,128)} %param.10) | copy-start | bytes 1156
  2.1 0.7 %copy-start.2 = (f32[3,8]{1,0:T(4,128)S(1)}, f32[3,8]{1,0:T(4,128)}, u32[]{:S(2)}) copy-start(f32[3,8]{1,0:T(4,128)} %constant.6.clone.coef_ref) | copy-start | bytes 292
  2.8 0.8 %copy-start = (f32[8,16,128]{2,1,0:T(8,128)S(1)}, f32[8,16,128]{2,1,0:T(8,128)}, u32[]{:S(2)}) copy-start(f32[8,16,128]{2,1,0:T(8,128)} %mass_ref.1) | copy-start | bytes 196612
  3.6 0.8 %copy-start.1 = (s32[8,16,128]{2,1,0:T(8,128)S(1)}, s32[8,16,128]{2,1,0:T(8,128)}, u32[]{:S(2)}) copy-start(s32[8,16,128]{2,1,0:T(8,128)} %act_ref.1) | copy-start | bytes 196612

commit v2 on v1

--- a/solution.py
+++ b/solution.py
@@ -119,6 +119,11 @@
         def _(device=device):
             pl.semaphore_signal(barrier, inc=1, device_id=device, device_id_type=MESH)
 
+    def spread(s, table):
+        for a in range(count_act):
+            tab_rows[s, a] = jnp.broadcast_to(table[:, a : a + 1], table.shape)
+
+    spread(0, table_ref[...])
     peers = 0
     for exists, _ in everyone:
         peers = peers + jnp.where(exists, 1, 0)
@@ -141,11 +146,6 @@
         def _(s=s, device=device):
             table_copy(s, device).start()
 
-    def spread(s, table):
-        for a in range(count_act):
-            tab_rows[s, a] = jnp.broadcast_to(table[:, a : a + 1], table.shape)
-
-    spread(0, table_ref[...])
     for s in range(1, windows):
         exists, device = later[s - 1]
         here, source = earlier[s - 1]
@@ -219,8 +219,8 @@
             )
         return made
 
-    def start(field, s, slot):
-        for exists, copy in copies(field, s, slot):
+    def start(field, s, slot, first=0, stop=6):
+        for exists, copy in copies(field, s, slot)[first:stop]:
 
             @pl.when(exists)
             def _(copy=copy):
@@ -294,13 +294,18 @@
                 half = vel[s, c, y] + kick * (force[c, y] * amp[s, n + 1, y] - stiff)
                 vel[s, c, y] = half
                 disp[other, s, c, y] = u + drift * half
+                if c == 2 and y == 0:
+
+                    @pl.when(n < STEPS - 1)
+                    def _():
+                        start(disp.at[other, s], s, other, 0, 1)
 
             finish(disp.at[slot, s], s, slot)
             stiffness(field, s, slot, use)
 
             @pl.when(n < STEPS - 1)
             def _(s=s):
-                start(disp.at[other, s], s, other)
+                start(disp.at[other, s], s, other, 1)
 
         return carry
 
@@ -342,13 +347,18 @@
 
                 def use(c, y, u, stiff, s=s):
                     cheb[other, s, c, y] = lead * (scale * stiff - u) - cheb[other, s, c, y]
+                    if c == 2 and y == 0:
+
+                        @pl.when(k < TERMS - 2)
+                        def _():
+                            start(cheb.at[other, s], s, 1 - wire, 0, 1)
 
                 finish(cheb.at[slot, s], s, wire)
                 stiffness(field, s, wire, use)
 
                 @pl.when(k < TERMS - 2)
                 def _(s=s):
-                    start(cheb.at[other, s], s, 1 - wire)
+                    start(cheb.at[other, s], s, 1 - wire, 1)
 
             return carry
 

time: 66 us -> 66.6 us (level)
  no operation moved by 1% of the time
where the time goes in v2:
time: 66.6 us; the launch traced here: 66.3 us
  Pallas kernels  61.1 us (92%)
  local copies, waits for them, and re-layouts  5.11 us (8%)
    pallas_call x1, Pallas kernels, body(): pl.pallas_call(functools.partial(kernel, counts + (windows, count_act)),...  61.1 us
    unnamed x11, local copies, waits for them, and re-layouts  4.33 us

profile of v2, /device:TPU:0, one launch (start us, length us, event | category | flops | bytes accessed | tf_op | source)
XLA Modules:
  0.0 66.3 jit_solution(11334120721249655876)
XLA Ops:
  0.0 0.0 copy-start.4
  0.0 0.7 copy-done.4
  0.7 0.8 %copy.8 = f32[9,16]{1,0:T(8,128)S(1)} copy(f32[9,16]{0,1:T(8,128)} %bitcast.2) | data formatting | bytes 1152 | tf_op jit(solution)/shard_map/transpose | solution.py:383
  1.4 0.0 copy-start.3
  1.4 0.1 select_reduce_fusion
  1.5 0.6 copy-done.3
  2.1 0.0 copy-start.2
  2.1 0.7 %copy-done.2 = f32[3,8]{1,0:T(4,128)S(1)} copy-done((f32[3,8]{1,0:T(4,128)S(1)}, f32[3,8]{1,0:T(4,128)}, u32[]{:S(2)}) %copy-start.2) | copy-done | bytes 120
  2.8 0.0 copy-start
  2.8 0.8 %copy-done = f32[8,16,128]{2,1,0:T(8,128)S(1)} copy-done((f32[8,16,128]{2,1,0:T(8,128)S(1)}, f32[8,16,128]{2,1,0:T(8,128)}, u32[]{:S(2)}) %copy-start) | copy-done | bytes 65560
  3.6 0.0 copy-start.1
  3.6 0.8 %copy-done.1 = s32[8,16,128]{2,1,0:T(8,128)S(1)} copy-done((s32[8,16,128]{2,1,0:T(8,128)S(1)}, s32[8,16,128]{2,1,0:T(8,128)}, u32[]{:S(2)}) %copy-start.1) | copy-done | bytes 65560
  4.5 61.1 %shard_map.67 = f32[1,6,8,16,128]{4,3,2,1,0:T(8,128)S(1)} custom-call(f32[8,16,128]{2,1,0:T(8,128)S(1)} %copy-done, s32[8,16,128]{2,1,0:T(8,128)S(1)} %copy-done.1, f32[16,128]{1,0:T(8,128)S(1)} %select_maximum_fusion.table_ref, f32[3,8]{1,0:T(4,128)S(1)} %copy-done.2), custom_call_target="tpu_custom_call" | custom-call | tf_op jit(solution)/shard_map/pallas_call | solution.py:392
  65.6 0.7 %copy.10 = f32[1,6,8,16,128]{4,3,2,1,0:T(8,128)} copy(f32[1,6,8,16,128]{4,3,2,1,0:T(8,128)S(1)} %shard_map.67) | data formatting | bytes 786432
  (2 shorter events, 0.0 us)
Async XLA Ops:
  0.0 0.7 copy-start.4
  1.4 0.7 %copy-start.3 = (f32[3,32]{1,0:T(4,128)S(1)}, f32[3,32]{1,0:T(4,128)}, u32[]{:S(2)}) copy-start(f32[3,32]{1,0:T(4,128)} %param.10) | copy-start | bytes 1156
  2.1 0.7 %copy-start.2 = (f32[3,8]{1,0:T(4,128)S(1)}, f32[3,8]{1,0:T(4,128)}, u32[]{:S(2)}) copy-start(f32[3,8]{1,0:T(4,128)} %constant.6.clone.coef_ref) | copy-start | bytes 292
  2.8 0.8 %copy-start = (f32[8,16,128]{2,1,0:T(8,128)S(1)}, f32[8,16,128]{2,1,0:T(8,128)}, u32[]{:S(2)}) copy-start(f32[8,16,128]{2,1,0:T(8,128)} %mass_ref.1) | copy-start | bytes 196612
  3.6 0.8 %copy-start.1 = (s32[8,16,128]{2,1,0:T(8,128)S(1)}, s32[8,16,128]{2,1,0:T(8,128)}, u32[]{:S(2)}) copy-start(s32[8,16,128]{2,1,0:T(8,128)} %act_ref.1) | copy-start | bytes 196612

commit v3 on v1

--- a/solution.py
+++ b/solution.py
@@ -12,6 +12,7 @@
 STEPS = 8
 TERMS = 8
 LANES = 128
+UNROLL = 4
 MESH = pl.DeviceIdType.MESH
 
 lame_ratio = 2.5
@@ -161,12 +162,11 @@
             table_copy(s, device).wait_send()
 
     times = STEPS + 1
-    entries = [(s, n) for s in range(windows) for n in range(times)]
-    entries += [(0, times + c) for c in range(3)]
-
-    def look_up(y, carry):
+    early = [(s, 0) for s in range(windows)] + [(0, times + c) for c in range(3)]
+    late = [(s, n) for s in range(windows) for n in range(1, times)]
+
+    def look_up(y, entries):
         act = act_ref[y]
-        mass = mass_ref[y]
 
         def one(a, values):
             hit = act == a
@@ -176,20 +176,26 @@
             )
 
         zero = jnp.zeros((size_z, size_x), jnp.float32)
-        values = lax.fori_loop(0, count_act, one, tuple(zero for _ in entries))
-        for (s, r), value in zip(entries, values):
-            if r < times:
-                amp[s, r, y] = value
+        start_values = tuple(zero for _ in entries)
+        return lax.fori_loop(0, count_act, one, start_values, unroll=UNROLL)
+
+    def first_step(y, carry):
+        values = look_up(y, early)
         for c in range(3):
-            force[c, y] = mass * values[windows * times + c]
+            force[c, y] = mass_ref[y] * values[windows + c]
         for s in range(windows):
             for c in range(3):
-                half = (0.5 * time_step) * (force[c, y] * values[s * times])
+                half = (0.5 * time_step) * (force[c, y] * values[s])
                 vel[s, c, y] = half
                 disp[0, s, c, y] = time_step * half
         return carry
 
-    lax.fori_loop(0, size_y, look_up, 0)
+    lax.fori_loop(0, size_y, first_step, 0)
+
+    def later_amplitudes(y, carry):
+        for (s, n), value in zip(late, look_up(y, late)):
+            amp[s, n, y] = value
+        return carry
 
     def copies(field, s, slot):
         top, end = size_y - 1, size_z - 1
@@ -306,6 +312,7 @@
 
     for s in range(windows):
         start(disp.at[0, s], s, 0)
+    lax.fori_loop(0, size_y, later_amplitudes, 0)
     lax.fori_loop(0, STEPS, forced, 0)
     final = STEPS % 2
 

time: 66 us -> 62.7 us (0.950)
  Pallas kernels: 60.5 us -> 57.1 us
    pallas_call x1, Pallas kernels: 60.5 us -> 57.1 us  [body(): pl.pallas_call(functools.partial(kernel, counts + (windows, count_act)),...]
where the time goes in v3:
time: 62.7 us; the launch traced here: 62.4 us
  Pallas kernels  57.1 us (91%)
  local copies, waits for them, and re-layouts  5.11 us (8%)
    pallas_call x1, Pallas kernels, body(): pl.pallas_call(functools.partial(kernel, counts + (windows, count_act)),...  57.1 us
    unnamed x11, local copies, waits for them, and re-layouts  4.33 us

profile of v3, /device:TPU:0, one launch (start us, length us, event | category | flops | bytes accessed | tf_op | source)
XLA Modules:
  0.0 62.4 jit_solution(17889700982018386383)
XLA Ops:
  0.0 0.0 copy-start.4
  0.0 0.7 %copy-done.4 = s32[1,32]{1,0:T(1,128)S(1)} copy-done((s32[1,32]{1,0:T(1,128)S(1)}, s32[1,32]{1,0:T(1,128)}, u32[]{:S(2)}) %copy-start.4) | copy-done | bytes 152
  0.7 0.8 %copy.8 = f32[9,16]{1,0:T(8,128)S(1)} copy(f32[9,16]{0,1:T(8,128)} %bitcast.2) | data formatting | bytes 1152 | tf_op jit(solution)/shard_map/transpose | solution.py:380
  1.4 0.0 copy-start.3
  1.4 0.1 select_reduce_fusion
  1.5 0.6 copy-done.3
  2.1 0.0 copy-start.2
  2.1 0.7 %copy-done.2 = f32[3,8]{1,0:T(4,128)S(1)} copy-done((f32[3,8]{1,0:T(4,128)S(1)}, f32[3,8]{1,0:T(4,128)}, u32[]{:S(2)}) %copy-start.2) | copy-done | bytes 120
  2.8 0.0 copy-start
  2.8 0.8 %copy-done = f32[8,16,128]{2,1,0:T(8,128)S(1)} copy-done((f32[8,16,128]{2,1,0:T(8,128)S(1)}, f32[8,16,128]{2,1,0:T(8,128)}, u32[]{:S(2)}) %copy-start) | copy-done | bytes 65560
  3.6 0.0 copy-start.1
  3.6 0.8 %copy-done.1 = s32[8,16,128]{2,1,0:T(8,128)S(1)} copy-done((s32[8,16,128]{2,1,0:T(8,128)S(1)}, s32[8,16,128]{2,1,0:T(8,128)}, u32[]{:S(2)}) %copy-start.1) | copy-done | bytes 65560
  4.5 57.1 %shard_map.67 = f32[1,6,8,16,128]{4,3,2,1,0:T(8,128)S(1)} custom-call(f32[8,16,128]{2,1,0:T(8,128)S(1)} %copy-done, s32[8,16,128]{2,1,0:T(8,128)S(1)} %copy-done.1, f32[16,128]{1,0:T(8,128)S(1)} %select_maximum_fusion.table_ref, f32[3,8]{1,0:T(4,128)S(1)} %copy-done.2), custom_call_target="tpu_custom_call" | custom-call | tf_op jit(solution)/shard_map/pallas_call | solution.py:389
  61.6 0.7 %copy.10 = f32[1,6,8,16,128]{4,3,2,1,0:T(8,128)} copy(f32[1,6,8,16,128]{4,3,2,1,0:T(8,128)S(1)} %shard_map.67) | data formatting | bytes 786432
  (2 shorter events, 0.0 us)
Async XLA Ops:
  0.0 0.7 %copy-start.4 = (s32[1,32]{1,0:T(1,128)S(1)}, s32[1,32]{1,0:T(1,128)}, u32[]{:S(2)}) copy-start(s32[1,32]{1,0:T(1,128)} %param.8) | copy-start | bytes 388
  1.4 0.7 %copy-start.3 = (f32[3,32]{1,0:T(4,128)S(1)}, f32[3,32]{1,0:T(4,128)}, u32[]{:S(2)}) copy-start(f32[3,32]{1,0:T(4,128)} %param.10) | copy-start | bytes 1156
  2.1 0.7 %copy-start.2 = (f32[3,8]{1,0:T(4,128)S(1)}, f32[3,8]{1,0:T(4,128)}, u32[]{:S(2)}) copy-start(f32[3,8]{1,0:T(4,128)} %constant.6.clone.coef_ref) | copy-start | bytes 292
  2.8 0.8 %copy-start = (f32[8,16,128]{2,1,0:T(8,128)S(1)}, f32[8,16,128]{2,1,0:T(8,128)}, u32[]{:S(2)}) copy-start(f32[8,16,128]{2,1,0:T(8,128)} %mass_ref.1) | copy-start | bytes 196612
  3.6 0.8 %copy-start.1 = (s32[8,16,128]{2,1,0:T(8,128)S(1)}, s32[8,16,128]{2,1,0:T(8,128)}, u32[]{:S(2)}) copy-start(s32[8,16,128]{2,1,0:T(8,128)} %act_ref.1) | copy-start | bytes 196612
